TPU v7x, 256 devices: a whole 4x4x8 slice. The times are simulated.
256 devices in a mesh: dp: 32 (over z, x), tensor: 8 (over y, core).
Axes of the slice: x: 4, y: 4, z: 8, core: 2. Of those that a mesh axis runs over, the one named last changes fastest.
Arguments:
- activations: bfloat16 [28672, 4096], P('dp', 'tensor'), may hold values from -6 to 6
- out_grads: bfloat16 [28672, 4096], P('dp', 'tensor'), may hold values from -6 to 6
- gate_act: bfloat16 [28672, 14336], P('dp', 'tensor'), may hold values from -6 to 6
- w_down: bfloat16 [14336, 4096], P('tensor', 'dp'), may hold values from -0.09375 to 0.09375
- proj_in: bfloat16 [4096, 64], P('tensor'), may hold values from -0.09375 to 0.09375
- proj_out: bfloat16 [14336, 64], P('tensor'), may hold values from -0.046875 to 0.046875
- lengths: int32 [32, 8], P('dp'), may hold values from 1 to 448, 896 in all within a row
- assign: int32 [256], replicated, may hold values from 0 to 255, each once
Outputs:
- loggrads: float32 [256, 64, 64], P('dp', 'tensor')
Inputs may be any that keep to these rules, and one draw needn't show every extreme that they name: `lengths`: each row gives the token counts of the 8 sequences packed into one data group's 896 rows and sums to 896. `assign`: a permutation of the sequence numbers.
All inputs are finite; a program needn't handle non-finite values.
Results may differ from a plain program's by a relative error of at most 0.013.
Values may be sent and summed in bfloat16 or wider, within the bound.
No kernel may reach another device: no remote copies, remote signals or barrier semaphores. Data moves between devices by JAX's collectives and lax.ppermute only.
A program may use at most 128 MiB of HBM per device.

v0:
```python
import jax
import jax.numpy as jnp
from jax import lax
from jax.sharding import PartitionSpec as P


def member_of(seq_lengths, tok_rows):
    slots = seq_lengths.shape[0]
    before = lax.iota(jnp.int32, slots)[None, :] < lax.iota(jnp.int32, slots)[:, None]
    starts = jnp.sum(jnp.where(before, seq_lengths[None, :], 0), axis=1)
    ends = starts + seq_lengths
    positions = lax.iota(jnp.int32, tok_rows)
    inside = (positions[None, :] >= starts[:, None]) & (positions[None, :] < ends[:, None])
    return jnp.where(inside, 1.0 / seq_lengths[:, None].astype(jnp.float32), 0.0)


def place(result, assign):
    slots, values = result.shape
    groups = lax.axis_size("dp")
    mine = lax.dynamic_slice_in_dim(assign, lax.axis_index("dp") * slots, slots, 0)
    placing = (mine[None, :] == lax.iota(jnp.int32, slots * groups)[:, None]).astype(jnp.bfloat16)
    spread = jnp.dot(placing, result, preferred_element_type=jnp.float32).astype(jnp.bfloat16)
    got = lax.all_to_all(spread, "dp", split_axis=0, concat_axis=0, tiled=True)
    return jnp.sum(got.reshape(groups, slots, values).astype(jnp.float32), axis=0)


def shards(activations, out_grads, gate_act, w_down, proj_in, proj_out, lengths, assign):
    tok_rows = activations.shape[0]
    rank_all = proj_in.shape[1]
    shard_count = lax.axis_size("tensor")
    slots = lengths.shape[1]
    cols = rank_all // shard_count
    in_part = jnp.dot(activations, proj_in, preferred_element_type=jnp.float32)
    in_high = in_part.astype(jnp.bfloat16)
    in_low = (in_part - in_high.astype(jnp.float32)).astype(jnp.bfloat16)
    full_grads = lax.all_gather(out_grads, "tensor", axis=1, tiled=True)
    in_all = lax.all_gather(jnp.concatenate([in_high, in_low], axis=1), "tensor", axis=0)
    in_all = jnp.sum(in_all.astype(jnp.float32), axis=0)
    in_sum = in_all[:, :rank_all] + in_all[:, rank_all:]
    weighted = member_of(lengths[0], tok_rows)[:, :, None] * in_sum[None, :, :]
    hidden_grad = lax.dot_general(
        full_grads,
        lax.all_gather(w_down, "dp", axis=1, tiled=True),
        (((1,), (1,)), ((), ())),
        preferred_element_type=jnp.float32,
    )
    up_grad = (hidden_grad * gate_act.astype(jnp.float32)).astype(jnp.bfloat16)
    out_part = jnp.dot(up_grad, proj_out, preferred_element_type=jnp.float32)
    part = jnp.einsum("ctp,tq->cpq", weighted, out_part, precision=lax.Precision.HIGHEST)
    part = part.reshape(slots, shard_count, cols * rank_all).transpose(1, 0, 2)
    result = jnp.sum(
        lax.all_to_all(part, "tensor", split_axis=0, concat_axis=0, tiled=True), axis=0
    )
    return place(result.astype(jnp.bfloat16), assign).reshape(slots, cols, rank_all)


def solution(mesh):
    in_specs = (
        P("dp", "tensor"),
        P("dp", "tensor"),
        P("dp", "tensor"),
        P("tensor", "dp"),
        P("tensor", None),
        P("tensor", None),
        P("dp", None),
        P(),
    )
    out_specs = P("dp", "tensor", None)
    return jax.shard_map(shards, mesh=mesh, in_specs=in_specs, out_specs=out_specs, check_vma=False)
```

profile of v0, /device:TPU:32, one launch (start us, length us, event | category | flops | bytes accessed | tf_op | source)
XLA Modules:
  0.0 291.1 jit_solution(1241002359419916471)
XLA Ops:
  6.5 0.0 copy-start
  6.5 0.0 all-gather.9.cloned.1.call-start
  6.5 1.2 copy-done
  7.7 1.3 subtract_convert_fusion
  9.0 0.7 pad_maximum_fusion
  9.7 0.0 all-gather.9.cloned.1.call-update
  9.7 0.0 all-gather.5.cloned.1.call-start
  9.8 0.7 all-gather.5.cloned.1.call-update
  10.5 0.0 all-gather.7.cloned.1.call-start
  10.5 0.7 all-gather.7.cloned.1.call-update
  11.2 0.8 select_reduce_fusion
  12.0 0.7 convert_divide_fusion
  12.7 0.7 bitcast_add_fusion
  13.3 0.1 fusion.9
  13.4 26.7 %all-gather.9.cloned.1.call-done = bf16[7168,128]{0,1:T(8,128)(2,1)} async-done(((bf16[896,128]{0,1:T(8,128)(2,1)}), bf16[7168,128]{0,1:T(8,128)(2,1)}) %all-gather.9.cloned.1.call-update) | async-done | bytes 1835024 | tf_op jit(solution)/shard_map/all_gather | solution.py:37
  40.1 1.9 convert_element_type.46
  42.0 0.0 copy-start.1
  42.0 0.6 copy.11
  42.7 0.9 bitcast_reduce_fusion
  43.6 0.0 copy-start.2
  43.6 46.3 %all-gather.5.cloned.1.call-done = bf16[896,4096]{1,0:T(8,128)(2,1)} async-done(((bf16[896,512]{1,0:T(8,128)(2,1)}), bf16[896,4096]{1,0:T(8,128)(2,1)}) %all-gather.5.cloned.1.call-update) | async-done | bytes 7340048 | tf_op jit(solution)/shard_map/all_gather | solution.py:36
  89.8 141.1 %all-gather.7.cloned.1.call-done = bf16[1792,4096]{1,0:T(8,128)(2,1)} async-done(((bf16[1792,128]{1,0:T(8,128)(2,1)}), bf16[1792,4096]{1,0:T(8,128)(2,1)}) %all-gather.7.cloned.1.call-update) | async-done | bytes 14680080 | tf_op jit(solution)/shard_map/all_gather | solution.py:43
  230.9 22.0 %fusion.4 = f32[896,64,1]{0,1,2:T(8,128)S(1)} fusion(bf16[1792,64]{0,1:T(8,128)(2,1)S(1)} %copy-done.1, bf16[896,1792]{1,0:T(8,128)(2,1)} %param.10, bf16[896,4096]{1,0:T(8,128)(2,1)} %all-gather.5.cloned.1.call-done, bf16[1792,4096]{1,0:T(8,128)(2,1)} %all-gather.7.cloned.1.call-done), kind=kOutput, calls=%fused_computation.7 | convolution fusion | flops 13363675136 | bytes 25690112 | tf_op jit(solution)/shard_map/dot_general | solution.py:48
  253.0 1.7 fusion.1
  254.6 0.1 reshape.85
  254.8 0.7 copy.13
  255.5 4.3 %all-to-all-start = ((f32[8,8,512]{2,1,0:T(8,128)}), f32[8,8,512]{2,1,0:T(8,128)S(1)}, u32[]{:S(2)}, u32[]{:S(2)}) async-start(f32[8,8,512]{2,1,0:T(8,128)} %bitcast.21), calls=%async_computation | async-start | bytes 262144 | tf_op jit(solution)/shard_map/all_to_all | solution.py:52
  259.8 0.1 dynamic_slice.3
  259.8 6.1 %all-to-all-done = f32[8,8,512]{2,1,0:T(8,128)S(1)} async-done(((f32[8,8,512]{2,1,0:T(8,128)}), f32[8,8,512]{2,1,0:T(8,128)S(1)}, u32[]{:S(2)}, u32[]{:S(2)}) %all-to-all-start) | async-done | bytes 131104 | tf_op jit(solution)/shard_map/all_to_all | solution.py:52
  265.9 0.2 fusion.3
  266.1 17.7 %all_to_all.14 = bf16[32,8,512]{2,1,0:T(8,128)(2,1)S(1)} all-to-all(bf16[32,8,512]{2,1,0:T(8,128)(2,1)S(1)} %fusion.3), channel_id=1, replica_groups=mesh['dp'=32,'tensor'=8] {'dp'}, dimensions={0} | all-to-all | bytes 524288 | tf_op jit(solution)/shard_map/all_to_all | solution.py:23
  283.9 0.7 reshape.86
  (5 shorter events, 0.1 us)
Async XLA Ops:
  6.5 1.2 copy-start
  6.5 33.6 %all-gather.9.cloned.1.call-start = ((), (), s32[]{:S(2)}) async-start(), calls=%async_computation.4 | async-start | bytes 2064384 | tf_op jit(solution)/shard_map/all_gather | solution.py:37
  9.7 80.1 %all-gather.5.cloned.1.call-start = ((), (), s32[]{:S(2)}) async-start(), calls=%async_computation.2 | async-start | bytes 8257536 | tf_op jit(solution)/shard_map/all_gather | solution.py:36
  10.5 220.4 %all-gather.7.cloned.1.call-start = ((), (), s32[]{:S(2)}) async-start(), calls=%async_computation.3 | async-start | bytes 15138816 | tf_op jit(solution)/shard_map/all_gather | solution.py:43
  42.0 188.9 %copy-start.1 = (bf16[1792,64]{0,1:T(8,128)(2,1)S(1)}, bf16[1792,64]{0,1:T(8,128)(2,1)}, u32[]{:S(2)}) copy-start(bf16[1792,64]{0,1:T(8,128)(2,1)} %param.13) | copy-start | bytes 688132
  43.6 216.2 %copy-start.2 = (s32[256]{0:T(256)S(1)}, s32[256]{0:T(256)}, u32[]{:S(2)}) copy-start(s32[256]{0:T(256)} %param.15) | copy-start | bytes 3076
  255.5 10.4 %all-to-all-start = ((f32[8,8,512]{2,1,0:T(8,128)}), f32[8,8,512]{2,1,0:T(8,128)S(1)}, u32[]{:S(2)}, u32[]{:S(2)}) async-start(f32[8,8,512]{2,1,0:T(8,128)} %bitcast.21), calls=%async_computation | async-start | bytes 262144 | tf_op jit(solution)/shard_map/all_to_all | solution.py:52
Sparse Core Ops, SparseCore 0:
  9.9 30.2 all-gather.8
  42.0 47.8 all-gather.4
  92.3 138.5 all-gather.6
where the time goes:
time: 291 us
  waiting for transfers between devices  222 us (76%)
  matrix products  25.2 us (9%)
  blocking collectives  17.7 us (6%)
  between operations  13.2 us (5%)
  other arithmetic  5.72 us (2%)
  starting transfers between devices  4.37 us (2%)
  local copies, waits for them, and re-layouts  3.43 us (1%)
    all_gather x1, waiting for transfers between devices, shards(): lax.all_gather(w_down, 'dp', axis=1, tiled=True)  141 us
    all_gather x1, waiting for transfers between devices, shards(): full_grads = lax.all_gather(out_grads, 'tensor', axis=1, tiled=True)  46.3 us
    all_gather x1, waiting for transfers between devices, shards(): lax.all_gather(jnp.concatenate([in_high, in_low], axis=1), 'tensor', axis=0)  26.7 us
    dot_general x1, matrix products, shards(): out_part = jnp.dot(up_grad, proj_out, preferred_element_type=jnp.float32)  22 us
    all_to_all x1, blocking collectives, place(): got = lax.all_to_all(spread, 'dp', split_axis=0, concat_axis=0, tiled=True)  17.7 us
    all_to_all x1, waiting for transfers between devices, shards(): lax.all_to_all(part, 'tensor', split_axis=0, concat_axis=0, tiled=True)  6.05 us
  transfers between devices with their start and end apart: 4, of which 4 were waited for; matrix products, arithmetic and copies ran while one was open for 2% of the time, Pallas kernels for 0%

commit v1 on v0

--- a/solution.py
+++ b/solution.py
@@ -33,7 +33,14 @@
     in_part = jnp.dot(activations, proj_in, preferred_element_type=jnp.float32)
     in_high = in_part.astype(jnp.bfloat16)
     in_low = (in_part - in_high.astype(jnp.float32)).astype(jnp.bfloat16)
-    full_grads = lax.all_gather(out_grads, "tensor", axis=1, tiled=True)
+    ring = [out_grads]
+    for hop in range(7):
+        ring.append(lax.ppermute(ring[-1], "tensor", [(dev, (dev + 1) % 8) for dev in range(8)]))
+    full_grads = jnp.roll(
+        jnp.concatenate(ring[::-1], axis=1),
+        (lax.axis_index("tensor") + 1) * ring[0].shape[1],
+        axis=1,
+    )
     in_all = lax.all_gather(jnp.concatenate([in_high, in_low], axis=1), "tensor", axis=0)
     in_all = jnp.sum(in_all.astype(jnp.float32), axis=0)
     in_sum = in_all[:, :rank_all] + in_all[:, rank_all:]

time: 291 us -> 243 us (0.84)
  waiting for transfers between devices: 222 us -> 147 us
  local copies, waits for them, and re-layouts: 3.43 us -> 29.2 us
    all_gather x1, waiting for transfers between devices: 141 us -> 39.6 us  [shards(): lax.all_gather(w_down, 'dp', axis=1, tiled=True)]
    ppermute x0 -> x7, waiting for transfers between devices: none -> 100 us  [shards(): lax.ppermute(ring[-1], 'tensor', [(dev, (dev + 1) % 8) for dev in range(8)])]
    all_gather x1 -> x0, waiting for transfers between devices: 46.3 us -> none  [shards(): full_grads = lax.all_gather(out_grads, 'tensor', axis=1, tiled=True)]
    all_gather x1, waiting for transfers between devices: 26.7 us -> 0.01 us  [shards(): lax.all_gather(jnp.concatenate([in_high, in_low], axis=1), 'tensor', axis=0)]
    unnamed x7 -> x36, local copies, waits for them, and re-layouts: 1.83 us -> 26.6 us
  transfers between devices with their start and end apart: 4 -> 10, of which waited for: 4 -> 9; matrix products, arithmetic and copies ran while one was open for 2% -> 12% of each run, Pallas kernels for 0% -> 0%
where the time goes in v1:
time: 243 us; the launch traced here: 242 us
  waiting for transfers between devices  147 us (60%)
  local copies, waits for them, and re-layouts  29.2 us (12%)
  matrix products  25.1 us (10%)
  blocking collectives  17.7 us (7%)
  between operations  13.5 us (6%)
  other arithmetic  5.88 us (2%)
  starting transfers between devices  4.37 us (2%)
    ppermute x7, waiting for transfers between devices, shards(): lax.ppermute(ring[-1], 'tensor', [(dev, (dev + 1) % 8) for dev in range(8)])  100 us
    all_gather x1, waiting for transfers between devices, shards(): lax.all_gather(w_down, 'dp', axis=1, tiled=True)  39.6 us
    unnamed x36, local copies, waits for them, and re-layouts  26.6 us
    dot_general x1, matrix products, shards(): out_part = jnp.dot(up_grad, proj_out, preferred_element_type=jnp.float32)  22 us
    all_to_all x1, blocking collectives, place(): got = lax.all_to_all(spread, 'dp', split_axis=0, concat_axis=0, tiled=True)  17.7 us
    all_to_all x1, waiting for transfers between devices, shards(): lax.all_to_all(part, 'tensor', split_axis=0, concat_axis=0, tiled=True)  6.05 us
  transfers between devices with their start and end apart: 10, of which 9 were waited for; matrix products, arithmetic and copies ran while one was open for 12% of the time, Pallas kernels for 0%

profile of v1, /device:TPU:32, one launch (start us, length us, event | category | flops | bytes accessed | tf_op | source)
XLA Modules:
  0.0 242.3 jit_solution(3343884244185471683)
XLA Ops:
  6.5 1.2 copy-done
  7.7 1.3 subtract_convert_fusion
  10.5 14.2 %collective-permute-done = bf16[896,512]{1,0:T(8,128)(2,1)S(1)} collective-permute-done((bf16[896,512]{1,0:T(8,128)(2,1)}, bf16[896,512]{1,0:T(8,128)(2,1)S(1)}, u32[]{:S(2)}, u32[]{:S(2)}) %collective-permute-start) | collective-permute-done | bytes 917536 | tf_op jit(solution)/shard_map/ppermute | solution.py:38
  24.7 20.9 %collective-permute-done.1 = bf16[896,512]{1,0:T(8,128)(2,1)S(1)} collective-permute-done((bf16[896,512]{1,0:T(8,128)(2,1)S(1)}, bf16[896,512]{1,0:T(8,128)(2,1)S(1)}, u32[]{:S(2)}, u32[]{:S(2)}) %collective-permute-start.1) | collective-permute-done | bytes 917536 | tf_op jit(solution)/shard_map/ppermute | solution.py:38
  45.6 14.0 %collective-permute-done.2 = bf16[896,512]{1,0:T(8,128)(2,1)S(1)} collective-permute-done((bf16[896,512]{1,0:T(8,128)(2,1)S(1)}, bf16[896,512]{1,0:T(8,128)(2,1)S(1)}, u32[]{:S(2)}, u32[]{:S(2)}) %collective-permute-start.2) | collective-permute-done | bytes 917536 | tf_op jit(solution)/shard_map/ppermute | solution.py:38
  60.6 14.0 %collective-permute-done.3 = bf16[896,512]{1,0:T(8,128)(2,1)S(1)} collective-permute-done((bf16[896,512]{1,0:T(8,128)(2,1)S(1)}, bf16[896,512]{1,0:T(8,128)(2,1)S(1)}, u32[]{:S(2)}, u32[]{:S(2)}) %collective-permute-start.3) | collective-permute-done | bytes 917536 | tf_op jit(solution)/shard_map/ppermute | solution.py:38
  75.6 14.1 %collective-permute-done.4 = bf16[896,512]{1,0:T(8,128)(2,1)} collective-permute-done((bf16[896,512]{1,0:T(8,128)(2,1)S(1)}, bf16[896,512]{1,0:T(8,128)(2,1)}, u32[]{:S(2)}, u32[]{:S(2)}) %collective-permute-start.4) | collective-permute-done | bytes 917536 | tf_op jit(solution)/shard_map/ppermute | solution.py:38
  91.2 12.9 %collective-permute-done.5 = bf16[896,512]{1,0:T(8,128)(2,1)} collective-permute-done((bf16[896,512]{1,0:T(8,128)(2,1)}, bf16[896,512]{1,0:T(8,128)(2,1)}, u32[]{:S(2)}, u32[]{:S(2)}) %collective-permute-start.5) | collective-permute-done | bytes 917536 | tf_op jit(solution)/shard_map/ppermute | solution.py:38
  104.9 2.0 convert_element_type.46
  108.5 9.9 %collective-permute-done.6 = bf16[896,512]{1,0:T(8,128)(2,1)} collective-permute-done((bf16[896,512]{1,0:T(8,128)(2,1)}, bf16[896,512]{1,0:T(8,128)(2,1)}, u32[]{:S(2)}, u32[]{:S(2)}) %collective-permute-start.6) | collective-permute-done | bytes 917536 | tf_op jit(solution)/shard_map/ppermute | solution.py:38
  118.4 2.3 constant_dynamic-update-slice_fusion.15
  120.7 2.2 constant_dynamic-update-slice_fusion.14
  122.9 2.2 constant_dynamic-update-slice_fusion.13
  125.1 1.1 constant_dynamic-update-slice_fusion.12
  126.2 1.0 constant_dynamic-update-slice_fusion.11
  127.2 1.1 constant_dynamic-update-slice_fusion.10
  128.3 1.1 constant_dynamic-update-slice_fusion.9
  129.3 1.1 constant_dynamic-update-slice_fusion.8
  130.4 2.3 constant_dynamic-update-slice_fusion.7
  132.7 2.3 constant_dynamic-update-slice_fusion.6
  135.0 2.2 constant_dynamic-update-slice_fusion.5
  137.2 1.0 constant_dynamic-update-slice_fusion.4
  138.2 1.0 constant_dynamic-update-slice_fusion.3
  139.2 1.0 constant_dynamic-update-slice_fusion.2
  140.2 1.0 constant_dynamic-update-slice_fusion.1
  141.2 1.0 constant_dynamic-update-slice_fusion
  142.3 39.6 %all-gather.4.cloned.1.call-done = bf16[1792,4096]{1,0:T(8,128)(2,1)} async-done(((bf16[1792,128]{1,0:T(8,128)(2,1)}), bf16[1792,4096]{1,0:T(8,128)(2,1)}) %all-gather.4.cloned.1.call-update) | async-done | bytes 14680080 | tf_op jit(solution)/shard_map/all_gather | solution.py:50
  181.9 22.0 %fusion.10 = f32[896,64,1]{0,1,2:T(8,128)S(1)} fusion(bf16[1792,64]{0,1:T(8,128)(2,1)S(1)} %copy-done.8, bf16[896,1792]{1,0:T(8,128)(2,1)} %param.10, bf16[1792,4096]{1,0:T(8,128)(2,1)} %all-gather.4.cloned.1.call-done, bf16[896,8192]{1,0:T(8,128)(2,1)} %constant_dynamic-update-slice_fusion, s32[]{:T(128)S(6)} %select_n.32), kind=kOutput, calls=%fused_computation.9 | convolution fusion | flops 13363675136 | bytes 25690116 | tf_op jit(solution)/shard_map/dot_general | solution.py:55
  203.9 1.6 fusion.7
  206.4 4.3 %all-to-all-start = ((f32[8,8,512]{2,1,0:T(8,128)}), f32[8,8,512]{2,1,0:T(8,128)S(1)}, u32[]{:S(2)}, u32[]{:S(2)}) async-start(f32[8,8,512]{2,1,0:T(8,128)} %bitcast.20), calls=%async_computation | async-start | bytes 262144 | tf_op jit(solution)/shard_map/all_to_all | solution.py:59
  210.8 6.1 %all-to-all-done = f32[8,8,512]{2,1,0:T(8,128)S(1)} async-done(((f32[8,8,512]{2,1,0:T(8,128)}), f32[8,8,512]{2,1,0:T(8,128)S(1)}, u32[]{:S(2)}, u32[]{:S(2)}) %all-to-all-start) | async-done | bytes 131104 | tf_op jit(solution)/shard_map/all_to_all | solution.py:59
  217.1 17.7 %all_to_all.14 = bf16[32,8,512]{2,1,0:T(8,128)(2,1)S(1)} all-to-all(bf16[32,8,512]{2,1,0:T(8,128)(2,1)S(1)} %fusion.9), channel_id=1, replica_groups=mesh['dp'=32,'tensor'=8] {'dp'}, dimensions={0} | all-to-all | bytes 524288 | tf_op jit(solution)/shard_map/all_to_all | solution.py:23
  (46 shorter events, 9.0 us)
Async XLA Ops:
  6.5 1.2 copy-start
  6.5 98.3 %all-gather.6.cloned.1.call-start = ((), (), s32[]{:S(2)}) async-start(), calls=%async_computation.3 | async-start | bytes 2064384 | tf_op jit(solution)/shard_map/all_gather | solution.py:44
  9.7 172.2 %all-gather.4.cloned.1.call-start = ((), (), s32[]{:S(2)}) async-start(), calls=%async_computation.2 | async-start | bytes 15138816 | tf_op jit(solution)/shard_map/all_gather | solution.py:50
  10.5 14.3 %collective-permute-start = (bf16[896,512]{1,0:T(8,128)(2,1)}, bf16[896,512]{1,0:T(8,128)(2,1)S(1)}, u32[]{:S(2)}, u32[]{:S(2)}) collective-permute-start(bf16[896,512]{1,0:T(8,128)(2,1)} %param.9), channel_id=1, source_target_pairs={{0,1},{1,2},{2,3},{3,4},{4,5},{5,6},{6,7},{7,0},{8,9},{9,10},{10,1... | collective-permute-start | bytes 2752520 | tf_op jit(solution)/shard_map/ppermute | solution.py:38
  24.7 20.9 %collective-permute-start.1 = (bf16[896,512]{1,0:T(8,128)(2,1)S(1)}, bf16[896,512]{1,0:T(8,128)(2,1)S(1)}, u32[]{:S(2)}, u32[]{:S(2)}) collective-permute-start(bf16[896,512]{1,0:T(8,128)(2,1)S(1)} %collective-permute-done), channel_id=1, source_target_pairs={{0,1},{1,2},{2,3},{3,4},{4,5},{5,6},{6,7},{7,0},{8,9},{9,10},{10,1... | collective-permute-start | bytes 2752520 | tf_op jit(solution)/shard_map/ppermute | solution.py:38
  45.6 59.1 %copy-start.2 = (bf16[896,512]{1,0:T(8,128)(2,1)}, bf16[896,512]{1,0:T(8,128)(2,1)S(1)}, u32[]{:S(2)}) copy-start(bf16[896,512]{1,0:T(8,128)(2,1)S(1)} %collective-permute-done.1) | copy-start | bytes 2752516
  45.6 14.0 %collective-permute-start.2 = (bf16[896,512]{1,0:T(8,128)(2,1)S(1)}, bf16[896,512]{1,0:T(8,128)(2,1)S(1)}, u32[]{:S(2)}, u32[]{:S(2)}) collective-permute-start(bf16[896,512]{1,0:T(8,128)(2,1)S(1)} %collective-permute-done.1), channel_id=1, source_target_pairs={{0,1},{1,2},{2,3},{3,4},{4,5},{5,6},{6,7},{7,0},{8,9},{9,10},{10,1... | collective-permute-start | bytes 2752520 | tf_op jit(solution)/shard_map/ppermute | solution.py:38
  59.7 1.0 copy-start.4
  60.6 14.0 %collective-permute-start.3 = (bf16[896,512]{1,0:T(8,128)(2,1)S(1)}, bf16[896,512]{1,0:T(8,128)(2,1)S(1)}, u32[]{:S(2)}, u32[]{:S(2)}) collective-permute-start(bf16[896,512]{1,0:T(8,128)(2,1)S(1)} %collective-permute-done.2), channel_id=1, source_target_pairs={{0,1},{1,2},{2,3},{3,4},{4,5},{5,6},{6,7},{7,0},{8,9},{9,10},{10,1... | collective-permute-start | bytes 2752520 | tf_op jit(solution)/shard_map/ppermute | solution.py:38
  74.6 0.9 copy-start.6
  75.6 14.1 %collective-permute-start.4 = (bf16[896,512]{1,0:T(8,128)(2,1)S(1)}, bf16[896,512]{1,0:T(8,128)(2,1)}, u32[]{:S(2)}, u32[]{:S(2)}) collective-permute-start(bf16[896,512]{1,0:T(8,128)(2,1)S(1)} %collective-permute-done.3), channel_id=1, source_target_pairs={{0,1},{1,2},{2,3},{3,4},{4,5},{5,6},{6,7},{7,0},{8,9},{9,10},{10,1... | collective-permute-start | bytes 2752520 | tf_op jit(solution)/shard_map/ppermute | solution.py:38
  89.7 14.3 %collective-permute-start.5 = (bf16[896,512]{1,0:T(8,128)(2,1)}, bf16[896,512]{1,0:T(8,128)(2,1)}, u32[]{:S(2)}, u32[]{:S(2)}) collective-permute-start(bf16[896,512]{1,0:T(8,128)(2,1)} %collective-permute-done.4), channel_id=1, source_target_pairs={{0,1},{1,2},{2,3},{3,4},{4,5},{5,6},{6,7},{7,0},{8,9},{9,10},{10,1... | collective-permute-start | bytes 2752520 | tf_op jit(solution)/shard_map/ppermute | solution.py:38
  104.1 14.3 %collective-permute-start.6 = (bf16[896,512]{1,0:T(8,128)(2,1)}, bf16[896,512]{1,0:T(8,128)(2,1)}, u32[]{:S(2)}, u32[]{:S(2)}) collective-permute-start(bf16[896,512]{1,0:T(8,128)(2,1)} %collective-permute-done.5), channel_id=1, source_target_pairs={{0,1},{1,2},{2,3},{3,4},{4,5},{5,6},{6,7},{7,0},{8,9},{9,10},{10,1... | collective-permute-start | bytes 2752520 | tf_op jit(solution)/shard_map/ppermute | solution.py:38
  104.8 24.5 %copy-start.1 = (bf16[896,512]{1,0:T(8,128)(2,1)S(1)}, bf16[896,512]{1,0:T(8,128)(2,1)}, u32[]{:S(2)}) copy-start(bf16[896,512]{1,0:T(8,128)(2,1)} %param.9) | copy-start | bytes 2752516
  104.8 20.3 %copy-start.7 = (bf16[896,512]{1,0:T(8,128)(2,1)S(1)}, bf16[896,512]{1,0:T(8,128)(2,1)}, u32[]{:S(2)}) copy-start(bf16[896,512]{1,0:T(8,128)(2,1)} %copy-done.6) | copy-start | bytes 2752516
  104.8 21.4 %copy-start.5 = (bf16[896,512]{1,0:T(8,128)(2,1)S(1)}, bf16[896,512]{1,0:T(8,128)(2,1)}, u32[]{:S(2)}) copy-start(bf16[896,512]{1,0:T(8,128)(2,1)} %copy-done.4) | copy-start | bytes 2752516
  104.8 22.4 %copy-start.3 = (bf16[896,512]{1,0:T(8,128)(2,1)S(1)}, bf16[896,512]{1,0:T(8,128)(2,1)}, u32[]{:S(2)}) copy-start(bf16[896,512]{1,0:T(8,128)(2,1)} %copy-done.2) | copy-start | bytes 2752516
  108.5 73.4 %copy-start.8 = (bf16[1792,64]{0,1:T(8,128)(2,1)S(1)}, bf16[1792,64]{0,1:T(8,128)(2,1)}, u32[]{:S(2)}) copy-start(bf16[1792,64]{0,1:T(8,128)(2,1)} %param.13) | copy-start | bytes 688132
  142.3 68.4 %copy-start.9 = (s32[256]{0:T(256)S(1)}, s32[256]{0:T(256)}, u32[]{:S(2)}) copy-start(s32[256]{0:T(256)} %param.15) | copy-start | bytes 3076
  206.4 10.4 %all-to-all-start = ((f32[8,8,512]{2,1,0:T(8,128)}), f32[8,8,512]{2,1,0:T(8,128)S(1)}, u32[]{:S(2)}, u32[]{:S(2)}) async-start(f32[8,8,512]{2,1,0:T(8,128)} %bitcast.20), calls=%async_computation | async-start | bytes 262144 | tf_op jit(solution)/shard_map/all_to_all | solution.py:59
Sparse Core Ops, SparseCore 0:
  9.8 31.2 all-gather.5
  43.6 138.2 all-gather.3
